TPU v7x, 256 devices: a whole 4x4x8 slice. The times are simulated.
256 devices in a mesh: dp: 32 (over z, y_hi, core), ctx: 8 (over x, y_lo).
Axes of the slice: x: 4, y: 4 (y_hi: 2, y_lo: 2; y = y_hi * 2 + y_lo), z: 8, core: 2. Of those that a mesh axis runs over, the one named last changes fastest.
Arguments:
- q_heads: bfloat16 [32, 1536, 2048], P('dp', 'ctx'), may hold values from -8 to 8
- keys: bfloat16 [32, 1536, 128], P('dp', 'ctx'), may hold values from -8 to 8
- values: bfloat16 [32, 1536, 128], P('dp', 'ctx'), may hold values from -6 to 6
- out_grad: bfloat16 [32, 1536, 2048], P('dp', 'ctx'), may hold values from -0.29882812 to 0.29882812
- hidden_in: bfloat16 [32, 1536, 16384], P('dp', 'ctx'), may hold values from -6 to 6
- doc_lengths: int32 [32, 8], P('dp'), may hold values from 1 to 576, 1536 in all within a row
- span_order: int32 [16], replicated, may hold values from 0 to 15, each once
- m_codes: int32 [16384, 256], P('dp'), may hold values from -127 to 127
- m_scales: float32 [2048], P('dp'), may hold values from 0.05 to 0.5
- v_codes: int32 [16384, 256], P('dp'), may hold values from 1 to 255
- v_scales: float32 [2048], P('dp'), may hold values from 0.05 to 1
Outputs:
- dq: bfloat16 [32, 1536, 2048], P('dp', 'ctx')
- update: float32 [16384, 256], P('dp')
- m_norm: float32 [16384, 256], P('dp')
- m_absmax: float32 [2048], P('dp')
- v_norm: float32 [16384, 256], P('dp')
- v_absmax: float32 [2048], P('dp')
Inputs may be any that keep to these rules, and one draw needn't show every extreme that they name: `doc_lengths`: each sequence's 8 lengths sum to 1536. `span_order`: each stored block names a different position block.
All inputs are finite; a program needn't handle non-finite values. Where the computation divides by a largest or mean magnitude, that divisor is 1e-20 or more.
Results may differ from a plain program's by a relative error of at most 0.0078.
Values may be sent and summed in bfloat16 or wider, within the bound.
A program may use at most 128 MiB of HBM per device.

v0:
```python
import math
import jax
import jax.numpy as jnp
from jax import lax
from jax.sharding import PartitionSpec as P

BLOCK = 2048
STEP = 10


def positions(order, span, total):
    rows = jnp.arange(total, dtype=jnp.int32)
    slot = rows // span
    match = slot[:, None] == jnp.arange(order.shape[0], dtype=jnp.int32)[None, :]
    first = jnp.sum(jnp.where(match, order[None, :], 0), axis=1)
    return first * span + rows % span


def documents(pos, lengths):
    index = jnp.arange(lengths.shape[0], dtype=jnp.int32)
    ends = jnp.sum(jnp.where(index[None, :] <= index[:, None], lengths[None, :], 0), axis=1)
    return jnp.sum((pos[:, None] >= ends[None, :]).astype(jnp.int32), axis=1)


def adam_blocks(grad, m_codes, m_scales, v_codes, v_scales):
    shape = grad.shape
    g_blocks = grad.reshape(-1, BLOCK)
    m_old = m_codes.reshape(-1, BLOCK).astype(jnp.float32) / 127.0 * m_scales[:, None]
    v_old = v_codes.reshape(-1, BLOCK).astype(jnp.float32) / 255.0 * v_scales[:, None]
    moment = 0.9 * m_old + 0.1 * g_blocks
    second = 0.95 * v_old + 0.05 * g_blocks * g_blocks
    update = moment / (1.0 - 0.9**STEP) / (jnp.sqrt(second / (1.0 - 0.95**STEP)) + 1e-08)
    m_absmax = jnp.max(jnp.abs(moment), axis=1)
    v_absmax = jnp.max(second, axis=1)
    m_norm = moment / (m_absmax[:, None] + 1e-06)
    v_norm = second / (v_absmax[:, None] + 1e-06)
    return (update.reshape(shape), m_norm.reshape(shape), m_absmax, v_norm.reshape(shape), v_absmax)


def contract_rows(left, right):
    return lax.dot_general(
        left, right, (((0,), (0,)), ((), ())), preferred_element_type=jnp.float32
    )


def contract_cols(left, right):
    return lax.dot_general(
        left, right, (((1,), (1,)), ((), ())), preferred_element_type=jnp.float32
    )


def shards(
    q_heads,
    keys,
    values,
    out_grad,
    hidden_in,
    doc_lengths,
    span_order,
    m_codes,
    m_scales,
    v_codes,
    v_scales,
):
    rows = q_heads.shape[1]
    head_dim = keys.shape[2]
    heads_width = q_heads.shape[2]
    nheads = heads_width // head_dim
    scale = 1.0 / math.sqrt(head_dim)
    total = rows * lax.axis_size("ctx")
    key_all, value_all = (
        lax.all_gather(keys[0], "ctx", axis=0, tiled=True),
        lax.all_gather(values[0], "ctx", axis=0, tiled=True),
    )
    pos = positions(span_order, rows // 2, total)
    doc = documents(pos, doc_lengths[0])
    first_row = lax.axis_index("ctx") * rows
    query_pos = lax.dynamic_slice_in_dim(pos, first_row, rows)
    query_doc = lax.dynamic_slice_in_dim(doc, first_row, rows)
    queries = q_heads[0].reshape(rows * nheads, head_dim)
    grads_out = out_grad[0].reshape(rows * nheads, head_dim)
    width = min(512, total)
    nblocks = total // width
    blocks = (
        key_all.reshape(nblocks, width, head_dim),
        value_all.reshape(nblocks, width, head_dim),
        pos.reshape(nblocks, width),
        doc.reshape(nblocks, width),
    )

    def block_masks(key_pos, key_doc):
        small = (key_pos[None, :] <= query_pos[:, None]) & (key_doc[None, :] == query_doc[:, None])
        wide = jnp.broadcast_to(small[:, None, :], (rows, nheads, width)).reshape(
            rows * nheads, width
        )
        return (small, wide)

    def forward_terms(carry, block):
        key_block, value_block, key_pos, key_doc = block
        small, wide = block_masks(key_pos, key_doc)
        top, denom, weighted = carry
        scores = contract_cols(queries, key_block) * scale
        dprob = contract_cols(grads_out, value_block)
        new_top = jnp.maximum(top, jnp.max(jnp.where(wide, scores, -1e30), axis=1, keepdims=True))
        expo = jnp.where(wide, jnp.exp(scores - new_top), 0.0)
        factor = jnp.exp(top - new_top)
        result = (
            new_top,
            denom * factor + jnp.sum(expo, axis=1, keepdims=True),
            weighted * factor + jnp.sum(expo * dprob, axis=1, keepdims=True),
        )
        return (result, None)

    column = jnp.zeros((rows * nheads, 1), jnp.float32)
    start_state = (column - 1e30, column, column)
    (top, denom, weighted), unused = lax.scan(forward_terms, start_state, blocks)
    delta = weighted / denom

    def backward_terms(accum, block):
        key_block, value_block, key_pos, key_doc = block
        small, wide = block_masks(key_pos, key_doc)
        acc = accum
        scores = contract_cols(queries, key_block) * scale
        dprob = contract_cols(grads_out, value_block)
        prob = jnp.where(wide, jnp.exp(scores - top), 0.0) / denom
        prob_low = prob.astype(jnp.bfloat16)
        dscore = (prob * (dprob - delta)).astype(jnp.bfloat16)
        acc = acc + jnp.dot(dscore, key_block, preferred_element_type=jnp.float32)
        dkey = contract_rows(dscore, queries) * scale
        dvalue = contract_rows(prob_low, grads_out)
        return (acc, jnp.concatenate([dkey, dvalue], axis=1))

    dq_sum, pieces = lax.scan(
        backward_terms, jnp.zeros((rows * nheads, head_dim), jnp.float32), blocks
    )
    dq = (dq_sum * scale).reshape(1, rows, heads_width).astype(jnp.bfloat16)
    partial_grads = pieces.reshape(total, 2 * head_dim)
    own = lax.psum_scatter(partial_grads, "ctx", scatter_dimension=0, tiled=True)
    own_low = own.astype(jnp.bfloat16)
    layer_in = hidden_in[0]
    grad = lax.psum_scatter(contract_rows(layer_in, own_low), "dp", scatter_dimension=0, tiled=True)
    grad = lax.psum(grad, "ctx")
    update, m_norm, m_absmax, v_norm, v_absmax = adam_blocks(
        grad, m_codes, m_scales, v_codes, v_scales
    )
    return (dq, update, m_norm, m_absmax, v_norm, v_absmax)


def solution(mesh):
    in_specs = (
        P("dp", "ctx", None),
        P("dp", "ctx", None),
        P("dp", "ctx", None),
        P("dp", "ctx", None),
        P("dp", "ctx", None),
        P("dp", None),
        P(),
        P("dp", None),
        P("dp"),
        P("dp", None),
        P("dp"),
    )
    out_specs = (
        P("dp", "ctx", None),
        P("dp", None),
        P("dp", None),
        P("dp"),
        P("dp", None),
        P("dp"),
    )
    return jax.shard_map(shards, mesh=mesh, in_specs=in_specs, out_specs=out_specs, check_vma=False)
```

profile of v0, /device:TPU:32, one launch (start us, length us, event | category | flops | bytes accessed | tf_op | source)
XLA Modules:
  0.0 549.0 jit_solution(25946978486925844)
XLA Ops:
  7.3 0.8 select_reduce_fusion
  8.1 0.8 select_reduce_fusion.1
  10.9 29.1 %all-gather = bf16[1,1536,128]{2,1,0:T(8,128)(2,1)S(1)} all-gather(bf16[1,192,128]{2,1,0:T(8,128)(2,1)} %param.16), channel_id=2, replica_groups=mesh['dp'=32,'ctx'=8] {'ctx'}, dimensions={1}, use_global_device_ids=true | all-gather | bytes 442368 | tf_op jit(solution)/shard_map/all_gather | solution.py:72
  40.0 1.4 reshape_squeeze.6
  41.5 30.8 %all-gather.1 = bf16[1,1536,128]{2,1,0:T(8,128)(2,1)} all-gather(bf16[1,192,128]{2,1,0:T(8,128)(2,1)} %param.17), channel_id=3, replica_groups=mesh['dp'=32,'ctx'=8] {'ctx'}, dimensions={1}, use_global_device_ids=true | all-gather | bytes 442368 | tf_op jit(solution)/shard_map/all_gather | solution.py:73
  72.7 46.8 %while.28 = (s32[]{:T(128)}, f32[3072,1]{0,1:T(1,128)}, f32[3072,1]{0,1:T(1,128)}, f32[3072,1]{0,1:T(1,128)}, s32[3,512]{1,0:T(4,128)}, /*index=5*/s32[192]{0:T(...) while((s32[]{:T(128)}, f32[3072,1]{0,1:T(1,128)}, ...), condition=%wide.region_7.8_spmd.clone, body=%wide.region_3.7_spmd.clone.sunk | while | flops 824497152 | bytes 55990092 | solution.py:116
  72.7 0.7 constant_dynamic-slice_fusion.6
  73.4 0.8 compare_and_fusion.4
  74.6 1.7 copy.45
  76.3 3.9 fusion.79
  80.2 5.2 fusion.81
  85.4 1.6 fusion.82
  87.8 0.7 constant_dynamic-slice_fusion.6
  88.5 0.8 compare_and_fusion.4
  89.8 1.7 copy.45
  91.5 3.9 fusion.79
  95.3 0.7 fusion.80
  96.0 5.2 fusion.81
  101.3 1.6 fusion.82
  104.4 0.8 compare_and_fusion.4
  105.6 1.7 copy.45
  107.3 3.8 fusion.79
  111.1 0.7 fusion.80
  111.9 5.2 fusion.81
  117.1 1.6 fusion.82
  119.5 1.3 div.70
  120.8 55.8 %while.29 = (s32[]{:T(128)}, f32[3072,128]{1,0:T(8,128)}, f32[3,512,256]{2,1,0:T(8,128)}, s32[3,512]{1,0:T(4,128)}, s32[192]{0:T(256)S(1)}, /*index=5*/s32[3,512...) while((s32[]{:T(128)}, f32[3072,128]{1,0:T(8,128)}, ...), condition=%wide.region_9.10_spmd.clone, body=%wide.region_8.9_spmd.clone.sunk | while | flops 2027126784 | bytes 108267456 | solution.py:133
  120.8 0.9 constant_dynamic-slice_fusion.7
  121.7 0.8 compare_and_fusion.5
  122.9 1.7 copy.46
  124.6 1.9 fusion.94
  126.6 2.9 fusion.95
  129.6 2.2 convolution_add_fusion.2
  131.8 1.1 copy-done.2
  132.9 2.3 fusion.96
  135.3 2.3 convolution_multiply_fusion.2
  137.8 0.8 constant_dynamic-update-slice_fusion.2
  139.1 0.9 constant_dynamic-slice_fusion.7
  140.0 0.8 compare_and_fusion.5
  141.2 1.7 copy.46
  143.0 1.9 fusion.94
  145.0 2.9 fusion.95
  147.9 3.8 convolution_add_fusion.2
  151.7 2.3 fusion.96
  154.0 2.3 convolution_multiply_fusion.2
  156.6 0.8 constant_dynamic-update-slice_fusion.2
  157.9 0.9 constant_dynamic-slice_fusion.7
  158.7 0.8 compare_and_fusion.5
  160.0 1.7 copy.46
  161.7 1.9 fusion.94
  163.7 2.9 fusion.95
  166.6 3.8 convolution_add_fusion.2
  170.4 2.3 fusion.96
  172.7 2.3 convolution_multiply_fusion.2
  175.3 0.8 constant_dynamic-update-slice_fusion.2
  176.7 49.4 %reduce-scatter.3.cloned.1.call-done = f32[192,256]{1,0:T(8,128)} async-done(((f32[1536,256]{1,0:T(8,128)}), f32[192,256]{1,0:T(8,128)}) %reduce-scatter.3.cloned.1.call-update) | async-done | bytes 196624 | tf_op jit(solution)/shard_map/reduce_scatter | solution.py:138
  226.1 11.0 %convolution_bitcast_fusion = f32[16384,256]{0,1:T(8,128)} fusion(bf16[1,192,16384]{2,1,0:T(8,128)(2,1)} %param.19, f32[192,256]{1,0:T(8,128)} %reduce-scatter.3.cloned.1.call-done), kind=kOutput, calls=%fused_computation.49 | convolution fusion | flops 1610661888 | bytes 23265280 | tf_op jit(solution)/shard_map/dot_general | solution.py:41
  237.2 218.4 %reduce-scatter.5.cloned.1.call-done = f32[512,256]{0,1:T(8,128)} async-done(((f32[16384,256]{0,1:T(8,128)}), f32[512,256]{0,1:T(8,128)}) %reduce-scatter.5.cloned.1.call-update) | async-done | bytes 524304 | tf_op jit(solution)/shard_map/reduce_scatter | solution.py:141
  455.8 1.2 convert_element_type.40
  457.8 79.3 %all-reduce.2.cloned.1.call-done = f32[512,256]{0,1:T(8,128)} async-done(((f32[512,256]{0,1:T(8,128)}), f32[512,256]{0,1:T(8,128)}) %all-reduce.2.cloned.1.call-update) | async-done | bytes 524304 | tf_op jit(solution)/shard_map/psum | solution.py:142
  537.2 1.3 abs_reduce_fusion
  539.5 1.0 copy.37
  540.5 1.0 copy.38
  541.5 1.0 copy.39
  (165 shorter events, 12.0 us)
Async XLA Ops:
  7.2 65.1 %copy-start.10 = (bf16[1,192,2048]{2,1,0:T(8,128)(2,1)S(1)}, bf16[1,192,2048]{2,1,0:T(8,128)(2,1)}, u32[]{:S(2)}) copy-start(bf16[1,192,2048]{2,1,0:T(8,128)(2,1)} %param.18) | copy-start | bytes 2359300
  7.2 218.9 %reduce-scatter.3.cloned.1.call-start = ((), (), s32[]{:S(2)}) async-start(), calls=%async_computation.2 | async-start | bytes 1769472 | tf_op jit(solution)/shard_map/reduce_scatter | solution.py:138
  80.2 5.2 copy-start
  85.4 1.7 copy-start.8
  85.4 1.7 copy-start.14
  85.4 1.7 copy-start.17
  87.2 0.6 copy-start.15
  87.2 0.6 copy-start.18
  96.0 5.2 copy-start
  101.2 1.7 copy-start.8
  101.2 1.7 copy-start.14
  101.2 1.7 copy-start.17
  103.0 0.6 copy-start.15
  103.0 0.6 copy-start.18
  111.9 5.2 copy-start
  117.1 1.7 copy-start.8
  117.1 1.7 copy-start.14
  117.1 1.7 copy-start.17
  118.8 0.6 copy-start.15
  118.8 0.6 copy-start.18
  120.8 5.8 %copy-start.4 = (bf16[3072,128]{1,0:T(8,128)(2,1)}, bf16[3072,128]{1,0:T(8,128)(2,1)S(1)}, u32[]{:S(2)}) copy-start(bf16[3072,128]{1,0:T(8,128)(2,1)S(1)} %get-tuple-element.577) | copy-start | bytes 2359300 | tf_op jit(solution)/shard_map/while
  120.8 5.8 %copy-start.6 = (bf16[3072,128]{1,0:T(8,128)(2,1)}, bf16[3072,128]{1,0:T(8,128)(2,1)S(1)}, u32[]{:S(2)}) copy-start(bf16[3072,128]{1,0:T(8,128)(2,1)S(1)} %get-tuple-element.581) | copy-start | bytes 2359300 | tf_op jit(solution)/shard_map/while
  120.8 3.8 copy-start.9
  120.8 3.8 copy-start.16
  124.6 2.0 copy-start.13
  126.6 3.0 copy-start.1
  129.6 3.4 copy-start.2
  137.6 1.1 copy-start.5
  137.6 1.6 copy-start.7
  139.1 5.8 %copy-start.4 = (bf16[3072,128]{1,0:T(8,128)(2,1)}, bf16[3072,128]{1,0:T(8,128)(2,1)S(1)}, u32[]{:S(2)}) copy-start(bf16[3072,128]{1,0:T(8,128)(2,1)S(1)} %get-tuple-element.577) | copy-start | bytes 2359300 | tf_op jit(solution)/shard_map/while
  139.1 5.8 %copy-start.6 = (bf16[3072,128]{1,0:T(8,128)(2,1)}, bf16[3072,128]{1,0:T(8,128)(2,1)S(1)}, u32[]{:S(2)}) copy-start(bf16[3072,128]{1,0:T(8,128)(2,1)S(1)} %get-tuple-element.581) | copy-start | bytes 2359300 | tf_op jit(solution)/shard_map/while
  139.1 3.8 copy-start.9
  139.1 3.8 copy-start.16
  143.0 2.0 copy-start.13
  144.9 3.0 copy-start.1
  147.9 3.8 copy-start.2
  156.3 1.1 copy-start.5
  156.3 1.6 copy-start.7
  157.9 5.8 %copy-start.4 = (bf16[3072,128]{1,0:T(8,128)(2,1)}, bf16[3072,128]{1,0:T(8,128)(2,1)S(1)}, u32[]{:S(2)}) copy-start(bf16[3072,128]{1,0:T(8,128)(2,1)S(1)} %get-tuple-element.577) | copy-start | bytes 2359300 | tf_op jit(solution)/shard_map/while
  157.9 5.8 %copy-start.6 = (bf16[3072,128]{1,0:T(8,128)(2,1)}, bf16[3072,128]{1,0:T(8,128)(2,1)S(1)}, u32[]{:S(2)}) copy-start(bf16[3072,128]{1,0:T(8,128)(2,1)S(1)} %get-tuple-element.581) | copy-start | bytes 2359300 | tf_op jit(solution)/shard_map/while
  157.9 3.8 copy-start.9
  157.9 3.8 copy-start.16
  161.7 2.0 copy-start.13
  163.7 3.0 copy-start.1
  166.6 3.8 copy-start.2
  175.0 1.1 copy-start.5
  175.0 1.6 copy-start.7
  176.6 279.0 %reduce-scatter.5.cloned.1.call-start = ((), (), s32[]{:S(2)}) async-start(), calls=%async_computation.3 | async-start | bytes 17301504 | tf_op jit(solution)/shard_map/reduce_scatter | solution.py:141
  237.1 218.6 %copy-start.3 = (f32[3072,128]{1,0:T(8,128)S(1)}, f32[3072,128]{1,0:T(8,128)}, u32[]{:S(2)}) copy-start(f32[3072,128]{1,0:T(8,128)} %get-tuple-element.146) | copy-start | bytes 4718596
  237.1 219.9 %copy-start.21 = (f32[64]{0:T(128)S(1)}, f32[64]{0:T(128)}, u32[]{:S(2)}) copy-start(f32[64]{0:T(128)} %param.23) | copy-start | bytes 772
  237.2 220.1 %copy-start.11 = (s32[512,256]{1,0:T(8,128)S(1)}, s32[512,256]{1,0:T(8,128)}, u32[]{:S(2)}) copy-start(s32[512,256]{1,0:T(8,128)} %param.22) | copy-start | bytes 1572868
  237.2 220.3 %copy-start.22 = (f32[64]{0:T(128)S(1)}, f32[64]{0:T(128)}, u32[]{:S(2)}) copy-start(f32[64]{0:T(128)} %param.25) | copy-start | bytes 772
  237.2 220.4 %copy-start.12 = (s32[512,256]{1,0:T(8,128)S(1)}, s32[512,256]{1,0:T(8,128)}, u32[]{:S(2)}) copy-start(s32[512,256]{1,0:T(8,128)} %param.24) | copy-start | bytes 1572868
  237.2 300.0 %all-reduce.2.cloned.1.call-start = ((), (), s32[]{:S(2)}) async-start(), calls=%async_computation.4 | async-start | bytes 1048576 | tf_op jit(solution)/shard_map/psum | solution.py:142
  538.6 3.9 copy-start.19
  539.0 3.5 copy-start.20
Sparse Core Ops, SparseCore 0:
  176.7 49.3 reduce-scatter.2
  237.3 218.3 reduce-scatter.4
  458.5 78.6 all-reduce.1
where the time goes:
time: 550 us; the launch traced here: 549 us
  waiting for transfers between devices  347 us (63%)
  matrix products  76.2 us (14%)
  blocking collectives  59.9 us (11%)
  local copies, waits for them, and re-layouts  33.6 us (6%)
  other arithmetic  17.1 us (3%)
  between operations  14 us (3%)
    reduce_scatter x1, waiting for transfers between devices, shards(): lax.psum_scatter(contract_rows(layer_in, own_low), 'dp', scatter_dimensio...  218 us
    psum x1, waiting for transfers between devices, shards(): grad = lax.psum(grad, 'ctx')  79.3 us
    reduce_scatter x1, waiting for transfers between devices, shards(): lax.psum_scatter(partial_grads, 'ctx', scatter_dimension=0, tiled=True)  49.4 us
    dot_general x12, matrix products, contract_cols(): lax.dot_general(left, right, (((1,), (1,)), ((), ())), preferred_element_...  41.6 us
    all_gather x1, blocking collectives, shards(): lax.all_gather(values[0], 'ctx', axis=0, tiled=True)  30.8 us
    all_gather x1, blocking collectives, shards(): lax.all_gather(keys[0], 'ctx', axis=0, tiled=True)  29.1 us
    dot_general x7, matrix products, contract_rows(): lax.dot_general(left, right, (((0,), (0,)), ((), ())), preferred_element_...  24.8 us
  transfers between devices with their start and end apart: 3, of which 3 were waited for; matrix products, arithmetic and copies ran while one was open for 0% of the time, Pallas kernels for 0%

commit v1 on v0

--- a/solution.py
+++ b/solution.py
@@ -139,7 +139,7 @@
     own_low = own.astype(jnp.bfloat16)
     layer_in = hidden_in[0]
     grad = lax.psum_scatter(contract_rows(layer_in, own_low), "dp", scatter_dimension=0, tiled=True)
-    grad = lax.psum(grad, "ctx")
+    grad = jnp.sum(lax.all_gather(grad, "ctx"), axis=0)
     update, m_norm, m_absmax, v_norm, v_absmax = adam_blocks(
         grad, m_codes, m_scales, v_codes, v_scales
     )

time: 550 us -> 578 us (1.051)
  waiting for transfers between devices: 347 us -> 358 us
  matrix products: 76.2 us -> 83.3 us
  local copies, waits for them, and re-layouts: 33.6 us -> 39.5 us
    all_gather x0 -> x1, waiting for transfers between devices: none -> 90.1 us  [shards(): grad = jnp.sum(lax.all_gather(grad, 'ctx'), axis=0)]
    psum x1 -> x0, waiting for transfers between devices: 79.3 us -> none  [shards(): grad = lax.psum(grad, 'ctx')]
    dot_general x12, matrix products: 41.6 us -> 48.8 us  [contract_cols(): lax.dot_general(left, right, (((1,), (1,)), ((), ())), preferred_element_...]
    unnamed x21 -> x18, local copies, waits for them, and re-layouts: 3.42 us -> 10.4 us
  transfers between devices with their start and end apart: 3 -> 3, of which waited for: 3 -> 3; matrix products, arithmetic and copies ran while one was open for 0% -> 1% of each run, Pallas kernels for 0% -> 0%
where the time goes in v1:
time: 578 us; the launch traced here: 574 us
  waiting for transfers between devices  358 us (62%)
  matrix products  83.3 us (14%)
  blocking collectives  59.9 us (10%)
  local copies, waits for them, and re-layouts  39.5 us (7%)
  other arithmetic  18.8 us (3%)
  between operations  14 us (2%)
    reduce_scatter x1, waiting for transfers between devices, shards(): lax.psum_scatter(contract_rows(layer_in, own_low), 'dp', scatter_dimensio...  219 us
    all_gather x1, waiting for transfers between devices, shards(): grad = jnp.sum(lax.all_gather(grad, 'ctx'), axis=0)  90.1 us
    reduce_scatter x1, waiting for transfers between devices, shards(): lax.psum_scatter(partial_grads, 'ctx', scatter_dimension=0, tiled=True)  49.2 us
    dot_general x12, matrix products, contract_cols(): lax.dot_general(left, right, (((1,), (1,)), ((), ())), preferred_element_...  48.8 us
    all_gather x1, blocking collectives, shards(): lax.all_gather(values[0], 'ctx', axis=0, tiled=True)  30.8 us
    all_gather x1, blocking collectives, shards(): lax.all_gather(keys[0], 'ctx', axis=0, tiled=True)  29.1 us
    dot_general x7, matrix products, contract_rows(): lax.dot_general(left, right, (((0,), (0,)), ((), ())), preferred_element_...  24.8 us
  transfers between devices with their start and end apart: 3, of which 3 were waited for; matrix products, arithmetic and copies ran while one was open for 1% of the time, Pallas kernels for 0%

profile of v1, /device:TPU:32, one launch (start us, length us, event | category | flops | bytes accessed | tf_op | source)
XLA Modules:
  0.0 574.2 jit_solution(13586583594535981172)
XLA Ops:
  7.2 0.7 select_reduce_fusion
  8.0 0.8 select_reduce_fusion.1
  10.9 29.1 %all-gather = bf16[1,1536,128]{2,1,0:T(8,128)(2,1)S(1)} all-gather(bf16[1,192,128]{2,1,0:T(8,128)(2,1)} %param.16), channel_id=2, replica_groups=mesh['dp'=32,'ctx'=8] {'ctx'}, dimensions={1}, use_global_device_ids=true | all-gather | bytes 442368 | tf_op jit(solution)/shard_map/all_gather | solution.py:72
  39.9 2.2 reshape_squeeze.6
  42.1 30.8 %all-gather.1 = bf16[1,1536,128]{2,1,0:T(8,128)(2,1)} all-gather(bf16[1,192,128]{2,1,0:T(8,128)(2,1)} %param.17), channel_id=3, replica_groups=mesh['dp'=32,'ctx'=8] {'ctx'}, dimensions={1}, use_global_device_ids=true | all-gather | bytes 442368 | tf_op jit(solution)/shard_map/all_gather | solution.py:73
  72.9 2.2 reshape_squeeze.7
  75.2 50.5 %while.28 = (s32[]{:T(128)}, f32[3072,1]{0,1:T(1,128)S(1)}, f32[3072,1]{0,1:T(1,128)}, f32[3072,1]{0,1:T(1,128)S(1)}, s32[3,512]{1,0:T(4,128)}, /*index=5*/s32[1...) while((s32[]{:T(128)}, f32[3072,1]{0,1:T(1,128)S(1)}, ...), condition=%wide.region_7.8_spmd.clone, body=%wide.region_3.7_spmd.clone.sunk | while | flops 824497152 | bytes 55744192 | solution.py:116
  75.2 0.7 constant_dynamic-slice_fusion.6
  75.9 0.8 compare_and_fusion.4
  77.1 1.7 copy.46
  78.8 5.0 fusion.79
  83.9 5.4 fusion.81
  89.2 1.6 fusion.82
  91.6 0.7 constant_dynamic-slice_fusion.6
  92.3 0.8 compare_and_fusion.4
  93.5 1.7 copy.46
  95.2 5.0 fusion.79
  100.2 5.3 fusion.81
  105.6 1.6 fusion.82
  107.3 1.4 fusion.83
  109.3 0.8 compare_and_fusion.4
  110.6 1.7 copy.46
  112.3 5.0 fusion.79
  117.3 5.4 fusion.81
  122.7 1.6 fusion.82
  124.3 1.4 fusion.83
  125.7 1.3 div.70
  127.0 56.8 %while.29 = (s32[]{:T(128)}, f32[3072,128]{1,0:T(8,128)}, f32[3,512,256]{2,1,0:T(8,128)}, s32[3,512]{1,0:T(4,128)}, s32[192]{0:T(256)S(1)}, /*index=5*/s32[3,512...) while((s32[]{:T(128)}, f32[3072,128]{1,0:T(8,128)}, ...), condition=%wide.region_9.10_spmd.clone, body=%wide.region_8.9_spmd.clone.sunk | while | flops 2027126784 | bytes 95536888 | solution.py:133
  127.8 0.8 compare_and_fusion.5
  129.0 1.7 copy.47
  130.7 3.1 fusion.94
  133.8 2.8 fusion.95
  136.6 2.2 convolution_add_fusion.2
  138.8 1.2 copy-done.2
  140.0 2.3 fusion.96
  142.3 2.3 convolution_multiply_fusion.2
  144.9 0.8 constant_dynamic-update-slice_fusion.2
  146.4 0.8 compare_and_fusion.5
  147.7 1.7 copy.47
  149.4 3.1 fusion.94
  152.5 2.8 fusion.95
  155.3 3.7 convolution_add_fusion.2
  159.1 2.3 fusion.96
  161.4 2.3 convolution_multiply_fusion.2
  163.9 0.9 constant_dynamic-update-slice_fusion.2
  165.5 0.8 compare_and_fusion.5
  166.8 1.7 copy.47
  168.5 3.1 fusion.94
  171.6 2.8 fusion.95
  174.4 3.7 convolution_add_fusion.2
  178.1 2.3 fusion.96
  180.5 2.3 convolution_multiply_fusion.2
  183.0 0.8 constant_dynamic-update-slice_fusion.2
  183.9 49.2 %reduce-scatter.3.cloned.1.call-done = f32[192,256]{1,0:T(8,128)} async-done(((f32[1536,256]{1,0:T(8,128)}), f32[192,256]{1,0:T(8,128)}) %reduce-scatter.3.cloned.1.call-update) | async-done | bytes 196624 | tf_op jit(solution)/shard_map/reduce_scatter | solution.py:138
  233.1 11.0 %convolution_bitcast_fusion = f32[16384,256]{0,1:T(8,128)} fusion(bf16[1,192,16384]{2,1,0:T(8,128)(2,1)} %param.19, f32[192,256]{1,0:T(8,128)} %reduce-scatter.3.cloned.1.call-done), kind=kOutput, calls=%fused_computation.49 | convolution fusion | flops 1610661888 | bytes 23265280 | tf_op jit(solution)/shard_map/dot_general | solution.py:41
  244.4 218.7 %reduce-scatter.5.cloned.1.call-done = f32[512,256]{0,1:T(8,128)} async-done(((f32[16384,256]{0,1:T(8,128)}), f32[512,256]{0,1:T(8,128)}) %reduce-scatter.5.cloned.1.call-update) | async-done | bytes 524304 | tf_op jit(solution)/shard_map/reduce_scatter | solution.py:141
  463.3 1.2 convert_element_type.40
  465.1 1.2 copy.35
  466.3 90.1 %all-gather.5.cloned.1.call-done = f32[4096,256]{0,1:T(8,128)} async-done(((f32[512,256]{0,1:T(8,128)}), f32[4096,256]{0,1:T(8,128)}) %all-gather.5.cloned.1.call-update) | async-done | bytes 4194320 | tf_op jit(solution)/shard_map/all_gather | solution.py:142
  556.4 6.0 %copy.42 = f32[32,8,8,512]{3,2,1,0:T(8,128)S(1)} copy(f32[32,8,8,512]{3,1,2,0:T(8,128)} %bitcast.149) | data formatting | bytes 8388608
  562.4 1.0 bitcast_reduce_fusion
  564.7 1.0 copy.36
  565.7 1.0 copy.37
  566.7 1.0 copy.38
  (91 shorter events, 11.2 us)
Async XLA Ops:
  7.2 225.9 %reduce-scatter.3.cloned.1.call-start = ((), (), s32[]{:S(2)}) async-start(), calls=%async_computation.2 | async-start | bytes 1769472 | tf_op jit(solution)/shard_map/reduce_scatter | solution.py:138
  83.8 5.4 copy-start
  100.2 5.4 copy-start
  117.3 5.4 copy-start
  133.8 2.8 copy-start.1
  136.6 3.4 copy-start.2
  152.5 2.8 copy-start.1
  155.3 3.8 copy-start.2
  171.5 2.8 copy-start.1
  174.4 3.8 copy-start.2
  183.9 279.3 %reduce-scatter.5.cloned.1.call-start = ((), (), s32[]{:S(2)}) async-start(), calls=%async_computation.3 | async-start | bytes 17301504 | tf_op jit(solution)/shard_map/reduce_scatter | solution.py:141
  244.1 219.1 %copy-start.3 = (f32[3072,128]{1,0:T(8,128)S(1)}, f32[3072,128]{1,0:T(8,128)}, u32[]{:S(2)}) copy-start(f32[3072,128]{1,0:T(8,128)} %get-tuple-element.146) | copy-start | bytes 4718596
  244.1 220.4 %copy-start.7 = (f32[64]{0:T(128)S(1)}, f32[64]{0:T(128)}, u32[]{:S(2)}) copy-start(f32[64]{0:T(128)} %param.23) | copy-start | bytes 772
  244.1 220.6 %copy-start.4 = (s32[512,256]{1,0:T(8,128)S(1)}, s32[512,256]{1,0:T(8,128)}, u32[]{:S(2)}) copy-start(s32[512,256]{1,0:T(8,128)} %param.22) | copy-start | bytes 1572868
  244.1 220.8 %copy-start.8 = (f32[64]{0:T(128)S(1)}, f32[64]{0:T(128)}, u32[]{:S(2)}) copy-start(f32[64]{0:T(128)} %param.25) | copy-start | bytes 772
  244.2 312.3 %all-gather.5.cloned.1.call-start = ((), (), s32[]{:S(2)}) async-start(), calls=%async_computation.4 | async-start | bytes 4718592 | tf_op jit(solution)/shard_map/all_gather | solution.py:142
  563.8 3.9 copy-start.5
  564.2 3.5 copy-start.6
Sparse Core Ops, SparseCore 0:
  184.0 49.0 reduce-scatter.2
  244.2 218.8 reduce-scatter.4
  465.1 91.2 all-gather.4
